TPU v7x, 32 devices: a whole 2x2x4 slice. The times are simulated.
32 devices in a mesh: dp: 8 (over y, x, core), seq: 4 (over z).
Axes of the slice: x: 2, y: 2, z: 4, core: 2. Of those that a mesh axis runs over, the one named last changes fastest.
Arguments:
- tokens: bfloat16 [16, 1024, 512], P('dp', 'seq'), may hold values from -6 to 6
- memory: bfloat16 [16, 1024, 512], P('dp', 'seq'), may hold values from -6 to 6
- tgt_segments: int32 [16, 1024], P('dp'), may hold values from 0 to 2, as said below
- mem_segments: int32 [16, 1024], P('dp'), may hold values from 0 to 2, as said below
- cotangent: bfloat16 [16, 1024, 512], P('dp', 'seq'), may hold values from -6 to 6
- w_qkv: bfloat16 [512, 1536], replicated, may hold values from -0.25 to 0.25
- w_self_out: bfloat16 [512, 512], replicated, may hold values from -1.5 to 1.5
- w_cross_q: bfloat16 [512, 512], replicated, may hold values from -0.25 to 0.25
- w_cross_kv: bfloat16 [512, 1024], replicated, may hold values from -0.25 to 0.25
- w_cross_out: bfloat16 [512, 512], replicated, may hold values from -1.5 to 1.5
- w_up: bfloat16 [512, 2048], replicated, may hold values from -0.25 to 0.25
- w_down: bfloat16 [2048, 512], replicated, may hold values from -0.125 to 0.125
- ln1_gain: float32 [512], replicated, may hold values from 0.25 to 1.75
- ln1_bias: float32 [512], replicated, may hold values from -1.8 to 1.8
- ln2_gain: float32 [512], replicated, may hold values from 0.25 to 1.75
- ln2_bias: float32 [512], replicated, may hold values from -1.8 to 1.8
- ln3_gain: float32 [512], replicated, may hold values from 0.25 to 1.75
- ln3_bias: float32 [512], replicated, may hold values from -1.8 to 1.8
Outputs:
- output: bfloat16 [16, 1024, 512], P('dp', 'seq')
- grad_tokens: float32 [16, 1024, 512], P('dp', 'seq')
- grad_memory: float32 [16, 1024, 512], P('dp', 'seq')
- grad_w_qkv: float32 [512, 1536], replicated
- grad_w_self_out: float32 [512, 512], replicated
- grad_w_cross_q: float32 [512, 512], replicated
- grad_w_cross_kv: float32 [512, 1024], replicated
- grad_w_cross_out: float32 [512, 512], replicated
- grad_w_up: float32 [512, 2048], replicated
- grad_w_down: float32 [2048, 512], replicated
- grad_ln1_gain: float32 [512], replicated
- grad_ln1_bias: float32 [512], replicated
- grad_ln2_gain: float32 [512], replicated
- grad_ln2_bias: float32 [512], replicated
- grad_ln3_gain: float32 [512], replicated
- grad_ln3_bias: float32 [512], replicated
Inputs may be any that keep to these rules, and one draw needn't show every extreme that they name: `tgt_segments`: along a row the ids never fall and all three occur; document 1 begins within the row's first 256 positions and ends within its last 256. `mem_segments`: along a row the ids never fall and all three occur.
All inputs are finite; a program needn't handle non-finite values.
Results may differ from a plain program's by a relative error of at most 0.02.
Values may be sent and summed in bfloat16 or wider, within the bound.
No kernel may reach another device: no remote copies, remote signals or barrier semaphores. Data moves between devices by JAX's collectives and lax.ppermute only.
A program may use at most 128 MiB of HBM per device.

v0:
```python
import math
import jax
import jax.numpy as jnp
from jax import lax
from jax.sharding import PartitionSpec as P

HEAD_DIM = 64


def mat_dot(left, right):
    return jnp.dot(left, right, preferred_element_type=jnp.float32)


def left_dot(left, right):
    return lax.dot_general(
        left, right, (((0,), (0,)), ((), ())), preferred_element_type=jnp.float32
    )


def right_dot(left, right):
    return lax.dot_general(
        left, right, (((1,), (1,)), ((), ())), preferred_element_type=jnp.float32
    )


def layer_norm(values, gain, bias):
    centre = values - jnp.mean(values, axis=-1, keepdims=True)
    recip = lax.rsqrt(jnp.mean(centre * centre, axis=-1, keepdims=True) + 1e-05)
    normed = centre * recip
    return (normed * gain + bias, normed, recip)


def norm_back(grad_out, normed, recip, gain):
    grad_gain = jnp.sum(grad_out * normed, axis=0)
    grad_bias = jnp.sum(grad_out, axis=0)
    scaled = grad_out * gain
    grad_in = recip * (
        scaled
        - jnp.mean(scaled, axis=-1, keepdims=True)
        - normed * jnp.mean(scaled * normed, axis=-1, keepdims=True)
    )
    return (grad_in, grad_gain, grad_bias)


def causal_mask(segment_row):
    place = jnp.arange(segment_row.shape[0])
    return (place[None, :] <= place[:, None]) & (segment_row[:, None] == segment_row[None, :])


def cross_mask(tgt_row, mem_row):
    return tgt_row[:, None] == mem_row[None, :]


def masked_scores(queries, key_heads, allowed, score_scale):
    scores = (
        jnp.einsum("qhd,khd->hqk", queries, key_heads, preferred_element_type=jnp.float32)
        * score_scale
    )
    return jnp.where(allowed[None], scores, -1000000000.0)


def attend_forward(queries, key_heads, value_heads, allowed, score_scale):
    scores = masked_scores(queries, key_heads, allowed, score_scale)
    highest = jnp.max(scores, axis=-1, keepdims=True)
    expo = jnp.exp(scores - highest)
    total = jnp.sum(expo, axis=-1, keepdims=True)
    probs = (expo / total).astype(jnp.bfloat16)
    context = jnp.einsum("hqk,khd->qhd", probs, value_heads, preferred_element_type=jnp.float32)
    return (context.astype(jnp.bfloat16), highest + jnp.log(total))


def attend_backward(queries, key_heads, value_heads, log_total, d_context, allowed, score_scale):
    scores = masked_scores(queries, key_heads, allowed, score_scale)
    probs = jnp.exp(scores - log_total)
    d_values = jnp.einsum(
        "hqk,qhd->khd", probs.astype(jnp.bfloat16), d_context, preferred_element_type=jnp.float32
    ).astype(jnp.bfloat16)
    d_probs = jnp.einsum("qhd,khd->hqk", d_context, value_heads, preferred_element_type=jnp.float32)
    centre = jnp.sum(probs * d_probs, axis=-1, keepdims=True)
    d_scores = (probs * (d_probs - centre)).astype(jnp.bfloat16)
    d_queries = (
        jnp.einsum("hqk,khd->qhd", d_scores, key_heads, preferred_element_type=jnp.float32)
        * score_scale
    ).astype(jnp.bfloat16)
    d_keys = (
        jnp.einsum("hqk,qhd->khd", d_scores, queries, preferred_element_type=jnp.float32)
        * score_scale
    ).astype(jnp.bfloat16)
    return (d_queries, d_keys, d_values)


def body(
    tokens,
    memory,
    tgt_segments,
    mem_segments,
    cotangent,
    w_qkv,
    w_self_out,
    w_cross_q,
    w_cross_kv,
    w_cross_out,
    w_up,
    w_down,
    ln1_gain,
    ln1_bias,
    ln2_gain,
    ln2_bias,
    ln3_gain,
    ln3_bias,
):
    row_count, tok_local, model_width = tokens.shape
    mem_local = memory.shape[1]
    seq_parts = lax.axis_size("seq")
    head_share = model_width // seq_parts
    heads_here = head_share // HEAD_DIM
    seq_len = tgt_segments.shape[1]
    mem_len = mem_segments.shape[1]
    score_scale = 1.0 / math.sqrt(HEAD_DIM)
    token_total = row_count * tok_local
    flat_tokens = tokens.reshape(token_total, model_width)
    flat_memory = memory.reshape(row_count * mem_local, model_width)
    mixed_proj = (
        mat_dot(flat_tokens, w_qkv)
        .astype(jnp.bfloat16)
        .reshape(row_count, tok_local, 3, seq_parts, head_share)
    )
    self_heads = lax.all_to_all(mixed_proj, "seq", split_axis=3, concat_axis=1, tiled=True).reshape(
        row_count, seq_len, 3, heads_here, HEAD_DIM
    )
    memory_proj = (
        mat_dot(flat_memory, w_cross_kv)
        .astype(jnp.bfloat16)
        .reshape(row_count, mem_local, 2, seq_parts, head_share)
    )
    memory_heads = lax.all_to_all(
        memory_proj, "seq", split_axis=3, concat_axis=1, tiled=True
    ).reshape(row_count, mem_len, 2, heads_here, HEAD_DIM)
    self_q = self_heads[:, :, 0]
    self_k = self_heads[:, :, 1]
    self_v = self_heads[:, :, 2]
    memory_k = memory_heads[:, :, 0]
    memory_v = memory_heads[:, :, 1]

    def self_forward(row_item):
        queries, key_heads, value_heads, segment_row = row_item
        return attend_forward(
            queries, key_heads, value_heads, causal_mask(segment_row), score_scale
        )

    self_context, self_lse = lax.map(self_forward, (self_q, self_k, self_v, tgt_segments))
    self_back = lax.all_to_all(
        self_context.reshape(row_count, seq_len, 1, head_share),
        "seq",
        split_axis=1,
        concat_axis=2,
        tiled=True,
    )
    context_one = self_back.reshape(token_total, model_width)
    attn_one = mat_dot(context_one, w_self_out)
    norm_one, normed_one, recip_one = layer_norm(
        flat_tokens.astype(jnp.float32) + attn_one, ln1_gain, ln1_bias
    )
    norm_one_low = norm_one.astype(jnp.bfloat16)
    cross_proj = (
        mat_dot(norm_one_low, w_cross_q)
        .astype(jnp.bfloat16)
        .reshape(row_count, tok_local, 1, seq_parts, head_share)
    )
    cross_q = lax.all_to_all(cross_proj, "seq", split_axis=3, concat_axis=1, tiled=True).reshape(
        row_count, seq_len, heads_here, HEAD_DIM
    )

    def cross_forward(row_item):
        queries, key_heads, value_heads, tgt_row, mem_row = row_item
        return attend_forward(
            queries, key_heads, value_heads, cross_mask(tgt_row, mem_row), score_scale
        )

    cross_context, cross_lse = lax.map(
        cross_forward, (cross_q, memory_k, memory_v, tgt_segments, mem_segments)
    )
    cross_back = lax.all_to_all(
        cross_context.reshape(row_count, seq_len, 1, head_share),
        "seq",
        split_axis=1,
        concat_axis=2,
        tiled=True,
    )
    context_two = cross_back.reshape(token_total, model_width)
    attn_two = mat_dot(context_two, w_cross_out)
    norm_two, normed_two, recip_two = layer_norm(norm_one + attn_two, ln2_gain, ln2_bias)
    norm_two_low = norm_two.astype(jnp.bfloat16)
    pre_act = mat_dot(norm_two_low, w_up)
    sigma = jax.nn.sigmoid(pre_act)
    hidden_low = (pre_act * sigma).astype(jnp.bfloat16)
    fed = mat_dot(hidden_low, w_down)
    result, normed_three, recip_three = layer_norm(norm_two + fed, ln3_gain, ln3_bias)
    output = result.astype(jnp.bfloat16).reshape(row_count, tok_local, model_width)
    grad_out = cotangent.reshape(token_total, model_width).astype(jnp.float32)
    d_resid_three, d_gain_three, d_bias_three = norm_back(
        grad_out, normed_three, recip_three, ln3_gain
    )
    d_fed_low = d_resid_three.astype(jnp.bfloat16)
    grad_down = left_dot(hidden_low, d_fed_low)
    d_hidden = right_dot(d_fed_low, w_down)
    d_pre_low = (d_hidden * sigma * (1.0 + pre_act * (1.0 - sigma))).astype(jnp.bfloat16)
    grad_up = left_dot(norm_two_low, d_pre_low)
    d_norm_two = d_resid_three + right_dot(d_pre_low, w_up)
    d_resid_two, d_gain_two, d_bias_two = norm_back(d_norm_two, normed_two, recip_two, ln2_gain)
    d_attn_two = d_resid_two.astype(jnp.bfloat16)
    grad_cross_out = left_dot(context_two, d_attn_two)
    d_context_two = (
        right_dot(d_attn_two, w_cross_out)
        .astype(jnp.bfloat16)
        .reshape(row_count, tok_local, seq_parts, head_share)
    )
    d_cross_heads = lax.all_to_all(
        d_context_two, "seq", split_axis=2, concat_axis=1, tiled=True
    ).reshape(row_count, seq_len, heads_here, HEAD_DIM)

    def cross_backward(row_item):
        queries, key_heads, value_heads, log_total, d_context, tgt_row, mem_row = row_item
        return attend_backward(
            queries,
            key_heads,
            value_heads,
            log_total,
            d_context,
            cross_mask(tgt_row, mem_row),
            score_scale,
        )

    d_cross_q, d_mem_keys, d_mem_values = lax.map(
        cross_backward,
        (cross_q, memory_k, memory_v, cross_lse, d_cross_heads, tgt_segments, mem_segments),
    )
    d_memory_kv = jnp.stack((d_mem_keys, d_mem_values), axis=2).reshape(
        row_count, mem_len, 2, 1, head_share
    )
    back_query, back_memory = (
        lax.all_to_all(
            d_cross_q.reshape(row_count, seq_len, 1, 1, head_share),
            "seq",
            split_axis=1,
            concat_axis=3,
            tiled=True,
        ),
        lax.all_to_all(d_memory_kv, "seq", split_axis=1, concat_axis=3, tiled=True),
    )
    d_query_flat = back_query.reshape(token_total, model_width)
    d_memory_flat = back_memory.reshape(row_count * mem_local, 2 * model_width)
    grad_cross_q = left_dot(norm_one_low, d_query_flat)
    grad_cross_kv = left_dot(flat_memory, d_memory_flat)
    grad_memory = right_dot(d_memory_flat, w_cross_kv).reshape(row_count, mem_local, model_width)
    d_norm_one = d_resid_two + right_dot(d_query_flat, w_cross_q)
    d_resid_one, d_gain_one, d_bias_one = norm_back(d_norm_one, normed_one, recip_one, ln1_gain)
    d_attn_one = d_resid_one.astype(jnp.bfloat16)
    grad_self_out = left_dot(context_one, d_attn_one)
    d_context_one = (
        right_dot(d_attn_one, w_self_out)
        .astype(jnp.bfloat16)
        .reshape(row_count, tok_local, seq_parts, head_share)
    )
    d_self_heads = lax.all_to_all(
        d_context_one, "seq", split_axis=2, concat_axis=1, tiled=True
    ).reshape(row_count, seq_len, heads_here, HEAD_DIM)

    def self_backward(row_item):
        queries, key_heads, value_heads, log_total, d_context, segment_row = row_item
        return attend_backward(
            queries,
            key_heads,
            value_heads,
            log_total,
            d_context,
            causal_mask(segment_row),
            score_scale,
        )

    d_self_q, d_self_k, d_self_v = lax.map(
        self_backward, (self_q, self_k, self_v, self_lse, d_self_heads, tgt_segments)
    )
    d_mixed = jnp.stack((d_self_q, d_self_k, d_self_v), axis=2).reshape(
        row_count, seq_len, 3, 1, head_share
    )
    back_mixed = lax.all_to_all(d_mixed, "seq", split_axis=1, concat_axis=3, tiled=True).reshape(
        token_total, 3 * model_width
    )
    grad_qkv = left_dot(flat_tokens, back_mixed)
    grad_tokens = (d_resid_one + right_dot(back_mixed, w_qkv)).reshape(
        row_count, tok_local, model_width
    )
    summed = lax.psum(
        (
            grad_qkv,
            grad_self_out,
            grad_cross_q,
            grad_cross_kv,
            grad_cross_out,
            grad_up,
            grad_down,
            d_gain_one,
            d_bias_one,
            d_gain_two,
            d_bias_two,
            d_gain_three,
            d_bias_three,
        ),
        ("dp", "seq"),
    )
    return (
        output,
        grad_tokens,
        grad_memory,
        summed[0],
        summed[1],
        summed[2],
        summed[3],
        summed[4],
        summed[5],
        summed[6],
        summed[7],
        summed[8],
        summed[9],
        summed[10],
        summed[11],
        summed[12],
    )


def solution(mesh):
    return jax.shard_map(
        body,
        mesh=mesh,
        in_specs=(
            P("dp", "seq", None),
            P("dp", "seq", None),
            P("dp", None),
            P("dp", None),
            P("dp", "seq", None),
            P(),
            P(),
            P(),
            P(),
            P(),
            P(),
            P(),
            P(),
            P(),
            P(),
            P(),
            P(),
            P(),
        ),
        out_specs=(
            P("dp", "seq", None),
            P("dp", "seq", None),
            P("dp", "seq", None),
            P(),
            P(),
            P(),
            P(),
            P(),
            P(),
            P(),
            P(),
            P(),
            P(),
            P(),
            P(),
            P(),
        ),
        check_vma=False,
    )
```

profile of v0, /device:TPU:0, one launch (start us, length us, event | category | flops | bytes accessed | tf_op | source)
XLA Modules:
  0.0 717.0 jit_solution(7663693203559814328)
XLA Ops:
  7.2 3.8 convolution_convert_fusion
  11.0 3.9 reshape.401
  17.9 6.3 all-to-all-start
  24.2 37.1 %all-to-all-done = bf16[2,256,3,4,128]{4,1,2,0,3:T(8,128)(2,1)} async-done(((bf16[2,256,3,4,128]{4,1,2,0,3:T(8,128)(2,1)}), bf16[2,256,3,4,128]{4,1,2,0,3:T(8,128)(2,1)}, u32[]{:S(2)}, u32[]{:S(2)}) %all-to-all-start) | async-done | bytes 1572896 | tf_op jit(solution)/shard_map/all_to_all | solution.py:128
  61.3 3.8 copy.197
  65.0 3.8 reshape.402
  72.0 16.4 %while.52 = (s32[]{:T(128)}, bf16[2,1024,2,64]{1,3,2,0:T(8,128)(2,1)}, f32[2,2,1024,1]{2,1,3,0:T(2,128)S(1)}, bf16[2,1024,2,64]{1,3,2,0:T(8,128)(2,1)}, s32[2,10...) while((s32[]{:T(128)}, ...), condition=%wide.region_3.4_spmd, body=%wide.region_0.3_spmd.sunk | while | flops 565311488 | bytes 36780216 | solution.py:151
  90.7 4.1 all-to-all-start.1
  103.5 5.4 all-to-all-done.1
  108.9 4.3 all-to-all-start.2
  122.7 15.7 %all-to-all-done.2 = bf16[2,256,2,4,128]{4,2,1,0,3:T(2,128)(2,1)} async-done(((bf16[2,256,2,4,128]{4,2,1,0,3:T(2,128)(2,1)}), bf16[2,256,2,4,128]{4,2,1,0,3:T(2,128)(2,1)}, u32[]{:S(2)}, u32[]{:S(2)}) %all-to-all-start.2) | async-done | bytes 1048608 | tf_op jit(solution)/shard_map/all_to_all | solution.py:136
  138.4 4.4 all-to-all-start.3
  142.9 3.8 copy.202
  151.5 5.4 all-to-all-done.3
  162.1 18.5 %while.53 = (s32[]{:T(128)}, bf16[2,1024,2,64]{1,3,2,0:T(8,128)(2,1)}, f32[2,2,1024,1]{2,1,3,0:T(2,128)S(1)}, bf16[2,1024,2,64]{1,3,2,0:T(8,128)(2,1)}, s32[2,10...) while((s32[]{:T(128)}, ...), condition=%wide.region_9.10_spmd, body=%wide.region_6.9_spmd.sunk | while | flops 563214336 | bytes 36792512 | solution.py:180
  182.6 4.8 all-to-all-start.4
  189.4 12.1 %all-to-all-done.4 = bf16[2,1024,1,128]{3,0,2,1:T(2,128)(2,1)} async-done(((bf16[2,1024,1,128]{3,0,2,1:T(2,128)(2,1)}), bf16[2,1024,1,128]{3,0,2,1:T(2,128)(2,1)}, u32[]{:S(2)}, u32[]{:S(2)}) %all-to-all-start.4) | async-done | bytes 524320 | tf_op jit(solution)/shard_map/all_to_all | solution.py:183
  221.2 4.3 all-to-all-start.5
  225.5 14.1 %all-to-all-done.5 = bf16[2,256,4,128]{3,1,0,2:T(8,128)(2,1)} async-done(((bf16[2,256,4,128]{3,1,0,2:T(8,128)(2,1)}), bf16[2,256,4,128]{3,1,0,2:T(8,128)(2,1)}, u32[]{:S(2)}, u32[]{:S(2)}) %all-to-all-start.5) | async-done | bytes 524320 | tf_op jit(solution)/shard_map/all_to_all | solution.py:218
  246.6 27.1 %while.54 = (s32[]{:T(128)}, bf16[2,1024,2,64]{1,3,2,0:T(8,128)(2,1)}, bf16[2,1024,2,64]{1,3,2,0:T(8,128)(2,1)}, bf16[2,1024,2,64]{1,3,2,0:T(8,128)(2,1)}, bf16[...) while((s32[]{:T(128)}, ...), condition=%wide.region_20.21_spmd, body=%wide.region_18.20_spmd.sunk | while | flops 1375336448 | bytes 86594928 | solution.py:234
  275.1 16.4 %all_to_all.150 = bf16[2,1024,1,1,128]{4,0,3,2,1:T(2,128)(2,1)S(1)} all-to-all(bf16[2,1024,1,1,128]{4,0,3,2,1:T(2,128)(2,1)S(1)} %copy.210), channel_id=1, replica_groups=mesh['dp'=8,'seq'=4] {'seq'}, dimensions={1} | all-to-all | bytes 1048576 | tf_op jit(solution)/shard_map/all_to_all | solution.py:242
  296.0 4.1 all-to-all-start.7
  303.5 10.2 %all-to-all-done.7 = bf16[2,256,4,128]{3,1,0,2:T(8,128)(2,1)} async-done(((bf16[2,256,4,128]{3,1,0,2:T(8,128)(2,1)}), bf16[2,256,4,128]{3,1,0,2:T(8,128)(2,1)}, u32[]{:S(2)}, u32[]{:S(2)}) %all-to-all-start.7) | async-done | bytes 524320 | tf_op jit(solution)/shard_map/all_to_all | solution.py:265
  313.7 4.5 all-to-all-start.9
  323.4 27.0 %while.55 = (s32[]{:T(128)}, bf16[2,1024,2,64]{1,3,2,0:T(8,128)(2,1)}, bf16[2,1024,2,64]{1,3,2,0:T(8,128)(2,1)}, bf16[2,1024,2,64]{1,3,2,0:T(8,128)(2,1)}, bf16[...) while((s32[]{:T(128)}, ...), condition=%wide.region_25.26_spmd, body=%wide.region_23.25_spmd.sunk | while | flops 1377433600 | bytes 86582632 | solution.py:281
  353.2 5.0 copy.215
  358.2 5.1 all-to-all-start.8
  366.2 5.2 fusion.153
  383.1 16.2 %all-to-all-done.8 = bf16[2,1024,3,1,128]{4,0,3,2,1:T(2,128)(2,1)} async-done(((bf16[2,1024,3,1,128]{4,0,3,2,1:T(2,128)(2,1)}), bf16[2,1024,3,1,128]{4,0,3,2,1:T(2,128)(2,1)}, u32[]{:S(2)}, u32[]{:S(2)}) %all-to-all-start.8) | async-done | bytes 1572896 | tf_op jit(solution)/shard_map/all_to_all | solution.py:287
  409.5 40.1 %all-reduce = (f32[512]{0:T(512)}, f32[512]{0:T(512)}, f32[512]{0:T(512)}, f32[512]{0:T(512)}, f32[512]{0:T(512)}, /*index=5*/f32[512]{0:T(512)}) all-reduce(f32[512]{0:T(512)S(1)} %get-tuple-element.334, f32[512]{0:T(512)S(1)} %get-tuple-element.341, f32[512]{0:T(512)S(1)} %copy-done.74, ...), channel_id=1, replica_groups=mesh['dp'=8,'seq'=4] {'dp','seq'}, use_global_device_ids=true, to_apply=%region_34.35 | all-reduce | flops 3072 | bytes 24576 | tf_op jit(solution)/shard_map/psum | solution.py:294
  454.5 3.8 convolution_add_fusion.3
  458.3 234.8 %all-reduce.4.cloned.1.call-done = (f32[512,1536]{0,1:T(8,128)}, f32[512,512]{1,0:T(8,128)}, f32[512,512]{1,0:T(8,128)}, f32[512,1024]{0,1:T(8,128)}, f32[512,51...) async-done(((f32[512,1536]{0,1:T(8,128)}, f32[512,512]{1,0:T(8,128)}, f32[512,512]{1,0:T(8,128)}, f32[512,1024]{0,1:T(8,128)}, f32[512,512]{1,0:T(8,128)}, ...) | async-done | bytes 16777232 | tf_op jit(solution)/shard_map/psum | solution.py:294
  (357 shorter events, 218.6 us)
Async XLA Ops:
  7.2 198.6 %copy-start = (bf16[512,2048]{1,0:T(8,128)(2,1)S(1)}, bf16[512,2048]{1,0:T(8,128)(2,1)}, u32[]{:S(2)}) copy-start(bf16[512,2048]{1,0:T(8,128)(2,1)} %param.36) | copy-start | bytes 6291460
  17.9 43.4 %all-to-all-start = ((bf16[2,256,3,4,128]{4,1,2,0,3:T(8,128)(2,1)}), bf16[2,256,3,4,128]{4,1,2,0,3:T(8,128)(2,1)}, u32[]{:S(2)}, u32[]{:S(2)}) async-start(bf16[2,256,3,4,128]{4,1,2,0,3:T(8,128)(2,1)} %copy.196), calls=%async_computation | async-start | bytes 3145728 | tf_op jit(solution)/shard_map/all_to_all | solution.py:128
  88.4 15.1 %copy-start.5 = (bf16[2,1024,2,64]{1,3,2,0:T(8,128)(2,1)}, bf16[2,1024,2,64]{1,3,2,0:T(8,128)(2,1)S(1)}, u32[]{:S(2)}) copy-start(bf16[2,1024,2,64]{1,3,2,0:T(8,128)(2,1)S(1)} %get-tuple-element.855) | copy-start | bytes 1572868
  88.4 15.1 %copy-start.7 = (bf16[2,1024,2,64]{1,3,2,0:T(8,128)(2,1)}, bf16[2,1024,2,64]{1,3,2,0:T(8,128)(2,1)S(1)}, u32[]{:S(2)}) copy-start(bf16[2,1024,2,64]{1,3,2,0:T(8,128)(2,1)S(1)} %get-tuple-element.856) | copy-start | bytes 1572868
  88.4 15.1 %copy-start.59 = (f32[2,2,1024,1]{2,1,3,0:T(2,128)}, f32[2,2,1024,1]{2,1,3,0:T(2,128)S(1)}, u32[]{:S(2)}) copy-start(f32[2,2,1024,1]{2,1,3,0:T(2,128)S(1)} %get-tuple-element.796) | copy-start | bytes 49156
  90.7 18.2 %all-to-all-start.1 = ((bf16[2,1024,1,128]{3,0,2,1:T(2,128)(2,1)}), bf16[2,1024,1,128]{3,0,2,1:T(2,128)(2,1)}, u32[]{:S(2)}, u32[]{:S(2)}) async-start(bf16[2,1024,1,128]{3,0,2,1:T(2,128)(2,1)} %copy.198), calls=%async_computation.1 | async-start | bytes 1048576 | tf_op jit(solution)/shard_map/all_to_all | solution.py:152
  103.5 14.1 %copy-start.70 = (f32[512]{0:T(512)S(1)}, f32[512]{0:T(512)}, u32[]{:S(2)}) copy-start(f32[512]{0:T(512)} %param.38) | copy-start | bytes 6148
  103.5 14.1 %copy-start.76 = (f32[512]{0:T(512)S(1)}, f32[512]{0:T(512)}, u32[]{:S(2)}) copy-start(f32[512]{0:T(512)} %param.39) | copy-start | bytes 6148
  108.9 29.5 %all-to-all-start.2 = ((bf16[2,256,2,4,128]{4,2,1,0,3:T(2,128)(2,1)}), bf16[2,256,2,4,128]{4,2,1,0,3:T(2,128)(2,1)}, u32[]{:S(2)}, u32[]{:S(2)}) async-start(bf16[2,256,2,4,128]{4,2,1,0,3:T(2,128)(2,1)} %copy.201), calls=%async_computation.2 | async-start | bytes 2097152 | tf_op jit(solution)/shard_map/all_to_all | solution.py:136
  138.4 18.5 %all-to-all-start.3 = ((bf16[2,256,1,4,128]{4,1,0,2,3:T(8,128)(2,1)}), bf16[2,256,1,4,128]{4,1,0,2,3:T(8,128)(2,1)}, u32[]{:S(2)}, u32[]{:S(2)}) async-start(bf16[2,256,1,4,128]{4,1,0,2,3:T(8,128)(2,1)} %copy.203), calls=%async_computation.3 | async-start | bytes 1048576 | tf_op jit(solution)/shard_map/all_to_all | solution.py:170
  142.9 19.2 %copy-start.58 = (s32[2,1024]{1,0:T(2,128)S(1)}, s32[2,1024]{1,0:T(2,128)}, u32[]{:S(2)}) copy-start(s32[2,1024]{1,0:T(2,128)} %param.29) | copy-start | bytes 24580
  162.1 25.4 %copy-start.69 = (f32[512]{0:T(512)S(1)}, f32[512]{0:T(512)}, u32[]{:S(2)}) copy-start(f32[512]{0:T(512)} %param.42) | copy-start | bytes 6148
  182.6 23.2 %copy-start.65 = (f32[512]{0:T(512)S(1)}, f32[512]{0:T(512)}, u32[]{:S(2)}) copy-start(f32[512]{0:T(512)} %param.40) | copy-start | bytes 6148
  182.6 23.2 %copy-start.67 = (f32[512]{0:T(512)S(1)}, f32[512]{0:T(512)}, u32[]{:S(2)}) copy-start(f32[512]{0:T(512)} %param.41) | copy-start | bytes 6148
  182.6 18.9 %all-to-all-start.4 = ((bf16[2,1024,1,128]{3,0,2,1:T(2,128)(2,1)}), bf16[2,1024,1,128]{3,0,2,1:T(2,128)(2,1)}, u32[]{:S(2)}, u32[]{:S(2)}) async-start(bf16[2,1024,1,128]{3,0,2,1:T(2,128)(2,1)} %copy.205), calls=%async_computation.4 | async-start | bytes 1048576 | tf_op jit(solution)/shard_map/all_to_all | solution.py:183
  216.0 29.8 %copy-start.10 = (f32[512,512]{1,0:T(8,128)}, f32[512,512]{1,0:T(8,128)S(1)}, u32[]{:S(2)}) copy-start(f32[512,512]{1,0:T(8,128)S(1)} %subtract_multiply_fusion.1) | copy-start | bytes 3145732
  216.0 30.6 %copy-start.4 = (bf16[2,1024,2,64]{1,3,2,0:T(8,128)(2,1)S(1)}, bf16[2,1024,2,64]{1,3,2,0:T(8,128)(2,1)}, u32[]{:S(2)}) copy-start(bf16[2,1024,2,64]{1,3,2,0:T(8,128)(2,1)} %get-tuple-element.854) | copy-start | bytes 1572868
  216.0 30.6 %copy-start.9 = (bf16[2,1024,2,64]{1,3,2,0:T(8,128)(2,1)S(1)}, bf16[2,1024,2,64]{1,3,2,0:T(8,128)(2,1)}, u32[]{:S(2)}) copy-start(bf16[2,1024,2,64]{1,3,2,0:T(8,128)(2,1)} %get-tuple-element.857) | copy-start | bytes 1572868
  221.2 18.4 %all-to-all-start.5 = ((bf16[2,256,4,128]{3,1,0,2:T(8,128)(2,1)}), bf16[2,256,4,128]{3,1,0,2:T(8,128)(2,1)}, u32[]{:S(2)}, u32[]{:S(2)}) async-start(bf16[2,256,4,128]{3,1,0,2:T(8,128)(2,1)} %copy.208), calls=%async_computation.5 | async-start | bytes 1048576 | tf_op jit(solution)/shard_map/all_to_all | solution.py:218
  273.7 18.3 %copy-start.11 = (f32[512,512]{1,0:T(8,128)S(1)}, f32[512,512]{1,0:T(8,128)}, u32[]{:S(2)}) copy-start(f32[512,512]{1,0:T(8,128)} %copy-done.10) | copy-start | bytes 3145732
  296.0 17.8 %all-to-all-start.7 = ((bf16[2,256,4,128]{3,1,0,2:T(8,128)(2,1)}), bf16[2,256,4,128]{3,1,0,2:T(8,128)(2,1)}, u32[]{:S(2)}, u32[]{:S(2)}) async-start(bf16[2,256,4,128]{3,1,0,2:T(8,128)(2,1)} %copy.213), calls=%async_computation.7 | async-start | bytes 1048576 | tf_op jit(solution)/shard_map/all_to_all | solution.py:265
  301.4 21.9 %copy-start.6 = (bf16[2,1024,2,64]{1,3,2,0:T(8,128)(2,1)S(1)}, bf16[2,1024,2,64]{1,3,2,0:T(8,128)(2,1)}, u32[]{:S(2)}) copy-start(bf16[2,1024,2,64]{1,3,2,0:T(8,128)(2,1)} %copy-done.5) | copy-start | bytes 1572868
  301.4 21.9 %copy-start.8 = (bf16[2,1024,2,64]{1,3,2,0:T(8,128)(2,1)S(1)}, bf16[2,1024,2,64]{1,3,2,0:T(8,128)(2,1)}, u32[]{:S(2)}) copy-start(bf16[2,1024,2,64]{1,3,2,0:T(8,128)(2,1)} %copy-done.7) | copy-start | bytes 1572868
  301.5 21.9 %copy-start.60 = (f32[2,2,1024,1]{2,1,3,0:T(2,128)S(1)}, f32[2,2,1024,1]{2,1,3,0:T(2,128)}, u32[]{:S(2)}) copy-start(f32[2,2,1024,1]{2,1,3,0:T(2,128)} %copy-done.59) | copy-start | bytes 49156
  313.7 44.5 %all-to-all-start.9 = ((bf16[2,1024,2,1,128]{4,0,3,2,1:T(2,128)(2,1)}), bf16[2,1024,2,1,128]{4,0,3,2,1:T(2,128)(2,1)}, u32[]{:S(2)}, u32[]{:S(2)}) async-start(bf16[2,1024,2,1,128]{4,0,3,2,1:T(2,128)(2,1)} %copy.218), calls=%async_computation.9 | async-start | bytes 2097152 | tf_op jit(solution)/shard_map/all_to_all | solution.py:249
  350.4 13.3 %copy-start.12 = (f32[512,512]{1,0:T(8,128)S(1)}, f32[512,512]{1,0:T(8,128)}, u32[]{:S(2)}) copy-start(f32[512,512]{1,0:T(8,128)} %copy-done.10) | copy-start | bytes 3145732
  353.2 13.0 %copy-start.64 = (f32[512]{0:T(512)S(1)}, f32[512]{0:T(512)}, u32[]{:S(2)}) copy-start(f32[512]{0:T(512)} %copy-done.63) | copy-start | bytes 6148
  353.2 13.0 %copy-start.66 = (f32[512]{0:T(512)S(1)}, f32[512]{0:T(512)}, u32[]{:S(2)}) copy-start(f32[512]{0:T(512)} %param.40) | copy-start | bytes 6148
  353.2 13.0 %copy-start.68 = (f32[512]{0:T(512)S(1)}, f32[512]{0:T(512)}, u32[]{:S(2)}) copy-start(f32[512]{0:T(512)} %param.41) | copy-start | bytes 6148
  358.2 41.1 %all-to-all-start.8 = ((bf16[2,1024,3,1,128]{4,0,3,2,1:T(2,128)(2,1)}), bf16[2,1024,3,1,128]{4,0,3,2,1:T(2,128)(2,1)}, u32[]{:S(2)}, u32[]{:S(2)}) async-start(bf16[2,1024,3,1,128]{4,0,3,2,1:T(2,128)(2,1)} %copy.215), calls=%async_computation.8 | async-start | bytes 3145728 | tf_op jit(solution)/shard_map/all_to_all | solution.py:287
  363.3 329.8 %all-reduce.4.cloned.1.call-start = ((), (), s32[]{:S(2)}) async-start(), calls=%async_computation.10 | async-start | bytes 33554432 | tf_op jit(solution)/shard_map/psum | solution.py:294
  383.1 23.1 %copy-start.51 = (bf16[2,256,512]{2,1,0:T(8,128)(2,1)S(1)}, bf16[2,256,512]{2,1,0:T(8,128)(2,1)}, u32[]{:S(2)}) copy-start(bf16[2,256,512]{2,1,0:T(8,128)(2,1)} %param.26) | copy-start | bytes 1572868
  (79 other events, 247.0 us)
Sparse Core Ops, SparseCore 0:
  409.0 284.0 all-reduce.3
where the time goes:
time: 728 us; the launch traced here: 717 us
  waiting for transfers between devices  351 us (48%)
  local copies, waits for them, and re-layouts  112 us (15%)
  matrix products  105 us (14%)
  blocking collectives  56.5 us (8%)
  starting transfers between devices  42.4 us (6%)
  other arithmetic  33.6 us (5%)
  between operations  14.9 us (2%)
    psum x1, waiting for transfers between devices, body(): lax.psum((grad_qkv, grad_self_out, grad_cross_q, grad_cross_kv, grad_cros...  235 us
    psum x1, blocking collectives, body(): lax.psum((grad_qkv, grad_self_out, grad_cross_q, grad_cross_kv, grad_cros...  40.1 us
    all_to_all x1, waiting for transfers between devices, body(): lax.all_to_all(mixed_proj, 'seq', split_axis=3, concat_axis=1, tiled=True)  37.1 us
    unnamed x122, local copies, waits for them, and re-layouts  19.7 us
    dot_general x7, matrix products, left_dot(): lax.dot_general(left, right, (((0,), (0,)), ((), ())), preferred_element_...  19 us
    all_to_all x1, blocking collectives, body(): lax.all_to_all(d_cross_q.reshape(row_count, seq_len, 1, 1, head_share), '...  16.4 us
    all_to_all x1, waiting for transfers between devices, body(): lax.all_to_all(d_mixed, 'seq', split_axis=1, concat_axis=3, tiled=True)  16.2 us
    all_to_all x1, waiting for transfers between devices, body(): lax.all_to_all(memory_proj, 'seq', split_axis=3, concat_axis=1, tiled=True)  15.7 us
  transfers between devices with their start and end apart: 10, of which 9 were waited for; matrix products, arithmetic and copies ran while one was open for 14% of the time, Pallas kernels for 0%

commit v1 on v0

--- a/solution.py
+++ b/solution.py
@@ -291,24 +291,23 @@
     grad_tokens = (d_resid_one + right_dot(back_mixed, w_qkv)).reshape(
         row_count, tok_local, model_width
     )
-    summed = lax.psum(
-        (
-            grad_qkv,
-            grad_self_out,
-            grad_cross_q,
-            grad_cross_kv,
-            grad_cross_out,
-            grad_up,
-            grad_down,
-            d_gain_one,
-            d_bias_one,
-            d_gain_two,
-            d_bias_two,
-            d_gain_three,
-            d_bias_three,
-        ),
-        ("dp", "seq"),
-    )
+    summed = (
+        grad_qkv,
+        grad_self_out,
+        grad_cross_q,
+        grad_cross_kv,
+        grad_cross_out,
+        grad_up,
+        grad_down,
+        d_gain_one,
+        d_bias_one,
+        d_gain_two,
+        d_bias_two,
+        d_gain_three,
+        d_bias_three,
+    )
+    for over in ("seq", "dp"):
+        summed = lax.psum(summed, over)
     return (
         output,
         grad_tokens,

time: 728 us -> 1240 us (1.70)
  waiting for transfers between devices: 351 us -> 861 us
    psum x1 -> x2, waiting for transfers between devices: 235 us -> 744 us  [body(): summed = lax.psum(summed, over)]
    psum x1 -> x2, blocking collectives: 40.1 us -> 40.1 us  [body(): summed = lax.psum(summed, over)]
  transfers between devices with their start and end apart: 10 -> 11, of which waited for: 9 -> 10; matrix products, arithmetic and copies ran while one was open for 14% -> 8% of each run, Pallas kernels for 0% -> 0%
where the time goes in v1:
time: 1240 us; the launch traced here: 1230 us
  waiting for transfers between devices  861 us (69%)
  local copies, waits for them, and re-layouts  110 us (9%)
  matrix products  108 us (9%)
  blocking collectives  56.5 us (5%)
  starting transfers between devices  42.3 us (3%)
  other arithmetic  33.6 us (3%)
  between operations  14.9 us (1%)
    psum x2, waiting for transfers between devices, body(): summed = lax.psum(summed, over)  744 us
    psum x2, blocking collectives, body(): summed = lax.psum(summed, over)  40.1 us
    all_to_all x1, waiting for transfers between devices, body(): lax.all_to_all(mixed_proj, 'seq', split_axis=3, concat_axis=1, tiled=True)  37.1 us
  transfers between devices with their start and end apart: 11, of which 10 were waited for; matrix products, arithmetic and copies ran while one was open for 8% of the time, Pallas kernels for 0%

profile of v1, /device:TPU:0, one launch (start us, length us, event | category | flops | bytes accessed | tf_op | source)
XLA Modules:
  0.0 1227.7 jit_solution(15992454373807563648)
XLA Ops:
  7.2 3.8 convolution_convert_fusion
  11.0 3.9 reshape.401
  17.9 6.3 all-to-all-start
  24.2 37.1 %all-to-all-done = bf16[2,256,3,4,128]{4,1,2,0,3:T(8,128)(2,1)} async-done(((bf16[2,256,3,4,128]{4,1,2,0,3:T(8,128)(2,1)}), bf16[2,256,3,4,128]{4,1,2,0,3:T(8,128)(2,1)}, u32[]{:S(2)}, u32[]{:S(2)}) %all-to-all-start) | async-done | bytes 1572896 | tf_op jit(solution)/shard_map/all_to_all | solution.py:128
  65.0 3.8 reshape.402
  72.2 18.4 %while.52 = (s32[]{:T(128)}, bf16[2,1024,2,64]{1,3,2,0:T(8,128)(2,1)}, f32[2,2,1024,1]{2,1,3,0:T(2,128)S(1)}, bf16[2,1024,2,64]{1,3,2,0:T(8,128)(2,1)}, s32[2,10...) while((s32[]{:T(128)}, ...), condition=%wide.region_3.4_spmd, body=%wide.region_0.3_spmd.sunk | while | flops 565311488 | bytes 36780216 | solution.py:151
  92.6 4.1 all-to-all-start.1
  103.4 7.4 all-to-all-done.1
  110.8 4.2 all-to-all-start.2
  125.6 14.7 %all-to-all-done.2 = bf16[2,256,2,4,128]{4,2,1,0,3:T(2,128)(2,1)} async-done(((bf16[2,256,2,4,128]{4,2,1,0,3:T(2,128)(2,1)}), bf16[2,256,2,4,128]{4,2,1,0,3:T(2,128)(2,1)}, u32[]{:S(2)}, u32[]{:S(2)}) %all-to-all-start.2) | async-done | bytes 1048608 | tf_op jit(solution)/shard_map/all_to_all | solution.py:136
  140.4 4.4 all-to-all-start.3
  144.8 3.8 copy.202
  153.5 5.4 all-to-all-done.3
  164.0 18.5 %while.53 = (s32[]{:T(128)}, bf16[2,1024,2,64]{1,3,2,0:T(8,128)(2,1)}, f32[2,2,1024,1]{2,1,3,0:T(2,128)S(1)}, bf16[2,1024,2,64]{1,3,2,0:T(8,128)(2,1)}, s32[2,10...) while((s32[]{:T(128)}, ...), condition=%wide.region_9.10_spmd, body=%wide.region_6.9_spmd.sunk | while | flops 563214336 | bytes 36792512 | solution.py:180
  184.5 4.8 all-to-all-start.4
  191.3 12.1 all-to-all-done.4
  223.0 4.3 all-to-all-start.5
  227.4 14.0 %all-to-all-done.5 = bf16[2,256,4,128]{3,1,0,2:T(8,128)(2,1)} async-done(((bf16[2,256,4,128]{3,1,0,2:T(8,128)(2,1)}), bf16[2,256,4,128]{3,1,0,2:T(8,128)(2,1)}, u32[]{:S(2)}, u32[]{:S(2)}) %all-to-all-start.5) | async-done | bytes 524320 | tf_op jit(solution)/shard_map/all_to_all | solution.py:218
  248.3 27.1 %while.54 = (s32[]{:T(128)}, bf16[2,1024,2,64]{1,3,2,0:T(8,128)(2,1)}, bf16[2,1024,2,64]{1,3,2,0:T(8,128)(2,1)}, bf16[2,1024,2,64]{1,3,2,0:T(8,128)(2,1)}, bf16[...) while((s32[]{:T(128)}, ...), condition=%wide.region_20.21_spmd, body=%wide.region_18.20_spmd.sunk | while | flops 1375336448 | bytes 86594928 | solution.py:234
  276.8 16.4 %all_to_all.150 = bf16[2,1024,1,1,128]{4,0,3,2,1:T(2,128)(2,1)S(1)} all-to-all(bf16[2,1024,1,1,128]{4,0,3,2,1:T(2,128)(2,1)S(1)} %copy.210), channel_id=1, replica_groups=mesh['dp'=8,'seq'=4] {'seq'}, dimensions={1} | all-to-all | bytes 1048576 | tf_op jit(solution)/shard_map/all_to_all | solution.py:242
  297.7 4.1 all-to-all-start.7
  305.2 10.2 all-to-all-done.7
  315.4 4.5 all-to-all-start.9
  325.0 27.0 %while.55 = (s32[]{:T(128)}, bf16[2,1024,2,64]{1,3,2,0:T(8,128)(2,1)}, bf16[2,1024,2,64]{1,3,2,0:T(8,128)(2,1)}, bf16[2,1024,2,64]{1,3,2,0:T(8,128)(2,1)}, bf16[...) while((s32[]{:T(128)}, ...), condition=%wide.region_25.26_spmd, body=%wide.region_23.25_spmd.sunk | while | flops 1377433600 | bytes 86582632 | solution.py:281
  354.8 5.0 copy.215
  359.9 5.1 all-to-all-start.8
  367.9 5.2 fusion.153
  384.7 16.3 %all-to-all-done.8 = bf16[2,1024,3,1,128]{4,0,3,2,1:T(2,128)(2,1)} async-done(((bf16[2,1024,3,1,128]{4,0,3,2,1:T(2,128)(2,1)}), bf16[2,1024,3,1,128]{4,0,3,2,1:T(2,128)(2,1)}, u32[]{:S(2)}, u32[]{:S(2)}) %all-to-all-start.8) | async-done | bytes 1572896 | tf_op jit(solution)/shard_map/all_to_all | solution.py:287
  410.5 567.6 %all-reduce.9.cloned.1.call-done = (f32[512,1536]{0,1:T(8,128)}, f32[512,512]{1,0:T(8,128)}, f32[512,512]{1,0:T(8,128)}, f32[512,1024]{0,1:T(8,128)}, f32[512,51...) async-done(((f32[512,1536]{0,1:T(8,128)}, f32[512,512]{1,0:T(8,128)}, f32[512,512]{1,0:T(8,128)}, f32[512,1024]{0,1:T(8,128)}, f32[512,512]{1,0:T(8,128)}, ...) | async-done | bytes 16777232 | tf_op jit(solution)/shard_map/psum | solution.py:310
  978.9 16.0 %all-reduce.2 = (f32[512]{0:T(512)S(1)}, f32[512]{0:T(512)S(1)}, f32[512]{0:T(512)S(1)}, f32[512]{0:T(512)S(1)}, f32[512]{0:T(512)S(1)}, /*index=5*/f32[512]{0:T(512)S(1)}) all-reduce(f32[512]{0:T(512)S(1)} %get-tuple-element.334, f32[512]{0:T(512)S(1)} %get-tuple-element.341, ...), channel_id=1, replica_groups=mesh['dp'=8,'seq'=4] {'seq'}, use_global_device_ids=true, to_apply=%region_41.42 | all-reduce | flops 3072 | bytes 24576 | tf_op jit(solution)/shard_map/psum | solution.py:310
  994.9 24.1 %all-reduce = (f32[512]{0:T(512)}, f32[512]{0:T(512)}, f32[512]{0:T(512)}, f32[512]{0:T(512)}, f32[512]{0:T(512)}, /*index=5*/f32[512]{0:T(512)}) all-reduce(f32[512]{0:T(512)S(1)} %get-tuple-element.429, f32[512]{0:T(512)S(1)} %get-tuple-element.430, f32[512]{0:T(512)S(1)} %get-tuple-element.431, ...), channel_id=1, replica_groups=mesh['dp'=8,'seq'=4] {'dp'}, use_global_device_ids=true, to_apply=%region_42.43 | all-reduce | flops 3072 | bytes 24576 | tf_op jit(solution)/shard_map/psum | solution.py:310
  1027.6 176.3 %all-reduce.7.cloned.1.call-done = (f32[512,1536]{0,1:T(8,128)}, f32[512,512]{1,0:T(8,128)}, f32[512,512]{1,0:T(8,128)}, f32[512,1024]{0,1:T(8,128)}, f32[512,51...) async-done(((f32[512,1536]{0,1:T(8,128)}, f32[512,512]{1,0:T(8,128)}, f32[512,512]{1,0:T(8,128)}, f32[512,1024]{0,1:T(8,128)}, f32[512,512]{1,0:T(8,128)}, ...) | async-done | bytes 16777232 | tf_op jit(solution)/shard_map/psum | solution.py:310
  (355 shorter events, 226.8 us)
Async XLA Ops:
  7.2 200.5 %copy-start = (bf16[512,2048]{1,0:T(8,128)(2,1)S(1)}, bf16[512,2048]{1,0:T(8,128)(2,1)}, u32[]{:S(2)}) copy-start(bf16[512,2048]{1,0:T(8,128)(2,1)} %param.36) | copy-start | bytes 6291460
  17.9 43.4 %all-to-all-start = ((bf16[2,256,3,4,128]{4,1,2,0,3:T(8,128)(2,1)}), bf16[2,256,3,4,128]{4,1,2,0,3:T(8,128)(2,1)}, u32[]{:S(2)}, u32[]{:S(2)}) async-start(bf16[2,256,3,4,128]{4,1,2,0,3:T(8,128)(2,1)} %copy.196), calls=%async_computation | async-start | bytes 3145728 | tf_op jit(solution)/shard_map/all_to_all | solution.py:128
  92.6 18.2 %all-to-all-start.1 = ((bf16[2,1024,1,128]{3,0,2,1:T(2,128)(2,1)}), bf16[2,1024,1,128]{3,0,2,1:T(2,128)(2,1)}, u32[]{:S(2)}, u32[]{:S(2)}) async-start(bf16[2,1024,1,128]{3,0,2,1:T(2,128)(2,1)} %copy.198), calls=%async_computation.1 | async-start | bytes 1048576 | tf_op jit(solution)/shard_map/all_to_all | solution.py:152
  103.4 16.0 %copy-start.67 = (f32[512]{0:T(512)S(1)}, f32[512]{0:T(512)}, u32[]{:S(2)}) copy-start(f32[512]{0:T(512)} %param.38) | copy-start | bytes 6148
  103.4 16.0 %copy-start.73 = (f32[512]{0:T(512)S(1)}, f32[512]{0:T(512)}, u32[]{:S(2)}) copy-start(f32[512]{0:T(512)} %param.39) | copy-start | bytes 6148
  110.8 29.5 %all-to-all-start.2 = ((bf16[2,256,2,4,128]{4,2,1,0,3:T(2,128)(2,1)}), bf16[2,256,2,4,128]{4,2,1,0,3:T(2,128)(2,1)}, u32[]{:S(2)}, u32[]{:S(2)}) async-start(bf16[2,256,2,4,128]{4,2,1,0,3:T(2,128)(2,1)} %copy.201), calls=%async_computation.2 | async-start | bytes 2097152 | tf_op jit(solution)/shard_map/all_to_all | solution.py:136
  140.4 18.5 %all-to-all-start.3 = ((bf16[2,256,1,4,128]{4,1,0,2,3:T(8,128)(2,1)}), bf16[2,256,1,4,128]{4,1,0,2,3:T(8,128)(2,1)}, u32[]{:S(2)}, u32[]{:S(2)}) async-start(bf16[2,256,1,4,128]{4,1,0,2,3:T(8,128)(2,1)} %copy.203), calls=%async_computation.3 | async-start | bytes 1048576 | tf_op jit(solution)/shard_map/all_to_all | solution.py:170
  144.8 19.2 %copy-start.55 = (s32[2,1024]{1,0:T(2,128)S(1)}, s32[2,1024]{1,0:T(2,128)}, u32[]{:S(2)}) copy-start(s32[2,1024]{1,0:T(2,128)} %param.29) | copy-start | bytes 24580
  164.0 25.3 %copy-start.66 = (f32[512]{0:T(512)S(1)}, f32[512]{0:T(512)}, u32[]{:S(2)}) copy-start(f32[512]{0:T(512)} %param.42) | copy-start | bytes 6148
  184.5 23.1 %copy-start.62 = (f32[512]{0:T(512)S(1)}, f32[512]{0:T(512)}, u32[]{:S(2)}) copy-start(f32[512]{0:T(512)} %param.40) | copy-start | bytes 6148
  184.5 23.1 %copy-start.64 = (f32[512]{0:T(512)S(1)}, f32[512]{0:T(512)}, u32[]{:S(2)}) copy-start(f32[512]{0:T(512)} %param.41) | copy-start | bytes 6148
  184.5 18.8 %all-to-all-start.4 = ((bf16[2,1024,1,128]{3,0,2,1:T(2,128)(2,1)}), bf16[2,1024,1,128]{3,0,2,1:T(2,128)(2,1)}, u32[]{:S(2)}, u32[]{:S(2)}) async-start(bf16[2,1024,1,128]{3,0,2,1:T(2,128)(2,1)} %copy.205), calls=%async_computation.4 | async-start | bytes 1048576 | tf_op jit(solution)/shard_map/all_to_all | solution.py:183
  217.9 29.5 %copy-start.8 = (f32[512,512]{1,0:T(8,128)}, f32[512,512]{1,0:T(8,128)S(1)}, u32[]{:S(2)}) copy-start(f32[512,512]{1,0:T(8,128)S(1)} %subtract_multiply_fusion.1) | copy-start | bytes 3145732
  217.9 30.4 %copy-start.4 = (bf16[2,1024,2,64]{1,3,2,0:T(8,128)(2,1)S(1)}, bf16[2,1024,2,64]{1,3,2,0:T(8,128)(2,1)}, u32[]{:S(2)}) copy-start(bf16[2,1024,2,64]{1,3,2,0:T(8,128)(2,1)} %get-tuple-element.881) | copy-start | bytes 1572868
  217.9 30.4 %copy-start.7 = (bf16[2,1024,2,64]{1,3,2,0:T(8,128)(2,1)S(1)}, bf16[2,1024,2,64]{1,3,2,0:T(8,128)(2,1)}, u32[]{:S(2)}) copy-start(bf16[2,1024,2,64]{1,3,2,0:T(8,128)(2,1)} %get-tuple-element.884) | copy-start | bytes 1572868
  223.0 18.4 %all-to-all-start.5 = ((bf16[2,256,4,128]{3,1,0,2:T(8,128)(2,1)}), bf16[2,256,4,128]{3,1,0,2:T(8,128)(2,1)}, u32[]{:S(2)}, u32[]{:S(2)}) async-start(bf16[2,256,4,128]{3,1,0,2:T(8,128)(2,1)} %copy.208), calls=%async_computation.5 | async-start | bytes 1048576 | tf_op jit(solution)/shard_map/all_to_all | solution.py:218
  275.4 18.3 %copy-start.9 = (f32[512,512]{1,0:T(8,128)S(1)}, f32[512,512]{1,0:T(8,128)}, u32[]{:S(2)}) copy-start(f32[512,512]{1,0:T(8,128)} %copy-done.8) | copy-start | bytes 3145732
  297.7 17.8 %all-to-all-start.7 = ((bf16[2,256,4,128]{3,1,0,2:T(8,128)(2,1)}), bf16[2,256,4,128]{3,1,0,2:T(8,128)(2,1)}, u32[]{:S(2)}, u32[]{:S(2)}) async-start(bf16[2,256,4,128]{3,1,0,2:T(8,128)(2,1)} %copy.213), calls=%async_computation.7 | async-start | bytes 1048576 | tf_op jit(solution)/shard_map/all_to_all | solution.py:265
  303.1 21.9 %copy-start.5 = (bf16[2,1024,2,64]{1,3,2,0:T(8,128)(2,1)S(1)}, bf16[2,1024,2,64]{1,3,2,0:T(8,128)(2,1)}, u32[]{:S(2)}) copy-start(bf16[2,1024,2,64]{1,3,2,0:T(8,128)(2,1)} %get-tuple-element.882) | copy-start | bytes 1572868
  303.1 21.9 %copy-start.6 = (bf16[2,1024,2,64]{1,3,2,0:T(8,128)(2,1)S(1)}, bf16[2,1024,2,64]{1,3,2,0:T(8,128)(2,1)}, u32[]{:S(2)}) copy-start(bf16[2,1024,2,64]{1,3,2,0:T(8,128)(2,1)} %get-tuple-element.883) | copy-start | bytes 1572868
  303.1 21.8 %copy-start.57 = (f32[2,2,1024,1]{2,1,3,0:T(2,128)S(1)}, f32[2,2,1024,1]{2,1,3,0:T(2,128)}, u32[]{:S(2)}) copy-start(f32[2,2,1024,1]{2,1,3,0:T(2,128)} %copy-done.56) | copy-start | bytes 49156
  315.4 44.4 %all-to-all-start.9 = ((bf16[2,1024,2,1,128]{4,0,3,2,1:T(2,128)(2,1)}), bf16[2,1024,2,1,128]{4,0,3,2,1:T(2,128)(2,1)}, u32[]{:S(2)}, u32[]{:S(2)}) async-start(bf16[2,1024,2,1,128]{4,0,3,2,1:T(2,128)(2,1)} %copy.218), calls=%async_computation.9 | async-start | bytes 2097152 | tf_op jit(solution)/shard_map/all_to_all | solution.py:249
  352.0 13.3 %copy-start.10 = (f32[512,512]{1,0:T(8,128)S(1)}, f32[512,512]{1,0:T(8,128)}, u32[]{:S(2)}) copy-start(f32[512,512]{1,0:T(8,128)} %copy-done.8) | copy-start | bytes 3145732
  354.8 13.0 %copy-start.3 = (f32[512,512]{1,0:T(8,128)S(1)}, f32[512,512]{1,0:T(8,128)}, u32[]{:S(2)}) copy-start(f32[512,512]{1,0:T(8,128)} %copy-done.2) | copy-start | bytes 3145732
  354.8 13.0 %copy-start.59 = (f32[512]{0:T(512)S(1)}, f32[512]{0:T(512)}, u32[]{:S(2)}) copy-start(f32[512]{0:T(512)} %copy-done.58) | copy-start | bytes 6148
  354.8 13.0 %copy-start.61 = (f32[512]{0:T(512)S(1)}, f32[512]{0:T(512)}, u32[]{:S(2)}) copy-start(f32[512]{0:T(512)} %copy-done.60) | copy-start | bytes 6148
  354.8 13.0 %copy-start.63 = (f32[512]{0:T(512)S(1)}, f32[512]{0:T(512)}, u32[]{:S(2)}) copy-start(f32[512]{0:T(512)} %param.40) | copy-start | bytes 6148
  354.8 13.0 %copy-start.65 = (f32[512]{0:T(512)S(1)}, f32[512]{0:T(512)}, u32[]{:S(2)}) copy-start(f32[512]{0:T(512)} %param.41) | copy-start | bytes 6148
  359.9 41.1 %all-to-all-start.8 = ((bf16[2,1024,3,1,128]{4,0,3,2,1:T(2,128)(2,1)}), bf16[2,1024,3,1,128]{4,0,3,2,1:T(2,128)(2,1)}, u32[]{:S(2)}, u32[]{:S(2)}) async-start(bf16[2,1024,3,1,128]{4,0,3,2,1:T(2,128)(2,1)} %copy.215), calls=%async_computation.8 | async-start | bytes 3145728 | tf_op jit(solution)/shard_map/all_to_all | solution.py:287
  364.9 613.2 %all-reduce.9.cloned.1.call-start = ((), (), s32[]{:S(2)}) async-start(), calls=%async_computation.11 | async-start | bytes 33554432 | tf_op jit(solution)/shard_map/psum | solution.py:310
  384.7 23.1 %copy-start.49 = (bf16[2,256,512]{2,1,0:T(8,128)(2,1)S(1)}, bf16[2,256,512]{2,1,0:T(8,128)(2,1)}, u32[]{:S(2)}) copy-start(bf16[2,256,512]{2,1,0:T(8,128)(2,1)} %param.26) | copy-start | bytes 1572868
  410.5 793.3 %all-reduce.7.cloned.1.call-start = ((), (), s32[]{:S(2)}) async-start(), calls=%async_computation.10 | async-start | bytes 33554432 | tf_op jit(solution)/shard_map/psum | solution.py:310
  (77 other events, 229.5 us)
Sparse Core Ops, SparseCore 0:
  410.6 567.5 all-reduce.8
  983.3 220.4 all-reduce.6
